TPU v7x, 512 devices: a whole 4x4x16 slice. The times are simulated.
512 devices in a mesh: dp: 16 (over y, z_hi), head: 32 (over x, z_lo, core).
Axes of the slice: x: 4, y: 4, z: 16 (z_hi: 4, z_lo: 4; z = z_hi * 4 + z_lo), core: 2. Of those that a mesh axis runs over, the one named last changes fastest.
Arguments:
- queries: bfloat16 [16, 768, 12288], P('dp', None, 'head'), may hold values from -6 to 6
- key_rows: bfloat16 [16, 768, 512], P('dp', 'head'), may hold values from -6 to 6
- value_rows: bfloat16 [16, 768, 512], P('dp', 'head'), may hold values from -6 to 6
- upstream: bfloat16 [16, 768, 12288], P('dp', None, 'head'), may hold values from -6 to 6
- head_gate: float32 [192], P('head'), may hold values from 0.5 to 2
- slot_heads: int32 [192], P('head'), may hold values from 0 to 231, as said below
Outputs:
- query_grad: bfloat16 [16, 768, 12288], P('dp', None, 'head')
- key_grad: bfloat16 [16, 768, 512], P('dp', 'head')
- value_grad: bfloat16 [16, 768, 512], P('dp', 'head')
- gate_grad: float32 [192], P('head')
Inputs may be any that keep to these rules, and one draw needn't show every extreme that they name: `slot_heads`: distinct initial head numbers in an arbitrary order; slot j of the head index i is entry i * 6 + j.
All inputs are finite; a program needn't handle non-finite values.
Results may differ from a plain program's by a relative error of at most 0.035.
Values may be sent and summed in bfloat16 or wider, within the bound.
A program may use at most 64 MiB of HBM per device.

v0:
```python
import jax
import jax.numpy as jnp
from jax import lax
from jax.sharding import PartitionSpec as P

HEAD_DIM = 64
KV_HEADS = 8
GROUP_HEADS = 29


score_scale = 0.125


def pick_groups(head_groups, k_table):
    choose = (head_groups[:, None] == jnp.arange(KV_HEADS, dtype=jnp.int32)[None, :]).astype(
        k_table.dtype
    )
    grouped = k_table.reshape(k_table.shape[0], KV_HEADS, HEAD_DIM)
    return jnp.einsum("hg,sgd->hsd", choose, grouped, preferred_element_type=jnp.float32).astype(
        k_table.dtype
    )


def causal_scores(q_head, k_block):
    scores = score_scale * jnp.dot(q_head, k_block.T, preferred_element_type=jnp.float32)
    row_index = lax.broadcasted_iota(jnp.int32, scores.shape, 0)
    col_index = lax.broadcasted_iota(jnp.int32, scores.shape, 1)
    return jnp.where(row_index >= col_index, scores, -jnp.inf)


def spread_groups(choose, grads):
    return (choose[None, :, None] * grads[:, None, :]).reshape(grads.shape[0], KV_HEADS * HEAD_DIM)


def query_side(q_head, k_head, v_head, dy_head, gate_one):
    scores = causal_scores(q_head, k_head)
    row_max = jnp.max(scores, axis=1, keepdims=True)
    exponent = jnp.exp(scores - row_max)
    row_sum = jnp.sum(exponent, axis=1, keepdims=True)
    weights = exponent / row_sum
    weights_low = weights.astype(jnp.bfloat16)
    attended = jnp.dot(weights_low, v_head, preferred_element_type=jnp.float32)
    upstream_wide = dy_head.astype(jnp.float32)
    gate_term = jnp.sum(upstream_wide * attended)
    out_grad = (gate_one * upstream_wide).astype(jnp.bfloat16)
    row_delta = jnp.sum(out_grad.astype(jnp.float32) * attended, axis=1, keepdims=True)
    weight_grad = jnp.dot(out_grad, v_head.T, preferred_element_type=jnp.float32)
    score_grad = (weights * (weight_grad - row_delta)).astype(jnp.bfloat16)
    query_grad = (
        score_scale * jnp.dot(score_grad, k_head, preferred_element_type=jnp.float32)
    ).astype(jnp.bfloat16)
    return (weights_low, score_grad, out_grad, query_grad, gate_term, row_max, row_sum, row_delta)


def local(queries, key_rows, value_rows, upstream, head_gate, slot_heads):
    key_all, value_all = (
        lax.all_gather(key_rows[0], "head", axis=0, tiled=True),
        lax.all_gather(value_rows[0], "head", axis=0, tiled=True),
    )
    length = key_all.shape[0]
    local_heads = slot_heads.shape[0]
    head_groups = slot_heads // GROUP_HEADS
    choose_all = (head_groups[:, None] == jnp.arange(KV_HEADS, dtype=jnp.int32)[None, :]).astype(
        jnp.float32
    )
    q_heads = queries[0].reshape(length, local_heads, HEAD_DIM).transpose(1, 0, 2)
    dy_heads = upstream[0].reshape(length, local_heads, HEAD_DIM).transpose(1, 0, 2)
    k_heads = pick_groups(head_groups, key_all)
    v_heads = pick_groups(head_groups, value_all)
    zero_sums = jnp.zeros((length, KV_HEADS * HEAD_DIM), jnp.float32)

    def head_step(running, inputs):
        key_part, value_part = running
        q_head, k_head, v_head, dy_head, gate_one, choose = inputs
        outcome = query_side(q_head, k_head, v_head, dy_head, gate_one)
        weights_low, score_grad, out_grad, query_grad, gate_term = outcome[:5]
        key_grad = score_scale * jnp.dot(score_grad.T, q_head, preferred_element_type=jnp.float32)
        value_grad = jnp.dot(weights_low.T, out_grad, preferred_element_type=jnp.float32)
        return (
            (
                key_part + spread_groups(choose, key_grad),
                value_part + spread_groups(choose, value_grad),
            ),
            (query_grad, gate_term),
        )

    parts, outputs = lax.scan(
        head_step,
        (zero_sums, zero_sums),
        (q_heads, k_heads, v_heads, dy_heads, head_gate, choose_all),
    )
    query_grads, gate_terms = outputs
    key_sum, value_sum = (
        lax.psum_scatter(
            parts[0].astype(jnp.bfloat16), "head", scatter_dimension=0, tiled=True
        ).astype(jnp.float32),
        lax.psum_scatter(
            parts[1].astype(jnp.bfloat16), "head", scatter_dimension=0, tiled=True
        ).astype(jnp.float32),
    )
    gate_grad = lax.psum(gate_terms, "dp") / lax.axis_size("dp")
    query_grad = query_grads.transpose(1, 0, 2).reshape(length, local_heads * HEAD_DIM)[None]
    return (
        query_grad,
        key_sum.astype(jnp.bfloat16)[None],
        value_sum.astype(jnp.bfloat16)[None],
        gate_grad,
    )


def solution(mesh):
    in_specs = (
        P("dp", None, "head"),
        P("dp", "head", None),
        P("dp", "head", None),
        P("dp", None, "head"),
        P("head"),
        P("head"),
    )
    out_specs = (P("dp", None, "head"), P("dp", "head", None), P("dp", "head", None), P("head"))
    return jax.shard_map(local, mesh=mesh, in_specs=in_specs, out_specs=out_specs, check_vma=False)
```

profile of v0, /device:TPU:1, one launch (start us, length us, event | category | flops | bytes accessed | tf_op | source)
XLA Modules:
  0.0 501.0 jit_solution(8380430222314008792)
XLA Ops:
  8.1 2.1 copy.31
  11.2 49.0 %all-gather = bf16[1,768,512]{2,1,0:T(8,128)(2,1)S(1)} all-gather(bf16[1,24,512]{2,1,0:T(8,128)(2,1)S(1)} %copy-done.7), channel_id=2, replica_groups=mesh['dp'=16,'head'=32] {'head'}, dimensions={1}, use_global_device_ids=true | all-gather | bytes 811008 | tf_op jit(solution)/shard_map/all_gather | solution.py:57
  61.2 43.9 %all-gather.1 = bf16[1,768,512]{2,1,0:T(8,128)(2,1)} all-gather(bf16[1,24,512]{2,1,0:T(8,128)(2,1)S(1)} %copy-done.8), channel_id=3, replica_groups=mesh['dp'=16,'head'=32] {'head'}, dimensions={1}, use_global_device_ids=true | all-gather | bytes 811008 | tf_op jit(solution)/shard_map/all_gather | solution.py:58
  108.1 89.5 %while.17 = (s32[]{:T(128)}, f32[768,512]{0,1:T(8,128)}, f32[768,512]{0,1:T(8,128)S(1)}, bf16[6,768,64]{1,2,0:T(8,128)(2,1)}, f32[6]{0:T(128)S(1)}, /*index=5*/f...) while((s32[]{:T(128)}, f32[768,512]{0,1:T(8,128)}, ...), condition=%wide.region_5.6_spmd.clone, body=%wide.region_0.5_spmd.clone.sunk | while | flops 464434944 | bytes 45160896 | solution.py:87
  108.9 1.5 constant_dynamic-slice_fusion.4
  113.8 1.6 fusion.78
  118.6 1.5 convolution_multiply_fusion.3
  123.9 1.5 constant_dynamic-slice_fusion.4
  128.7 1.6 fusion.78
  133.5 1.5 convolution_multiply_fusion.3
  138.8 1.5 constant_dynamic-slice_fusion.4
  143.6 1.6 fusion.78
  148.4 1.5 convolution_multiply_fusion.3
  153.7 1.5 constant_dynamic-slice_fusion.4
  158.5 1.6 fusion.78
  168.6 1.5 constant_dynamic-slice_fusion.4
  173.4 1.6 fusion.78
  183.5 1.5 constant_dynamic-slice_fusion.4
  188.3 1.6 fusion.78
  193.2 1.5 convolution_multiply_fusion.3
  197.6 2.6 copy.40
  201.5 49.6 %psum.7 = f32[6]{0:T(128)S(1)} all-reduce(f32[6]{0:T(128)S(1)} %get-tuple-element.67), channel_id=1, replica_groups=mesh['dp'=16,'head'=32] {'dp'}, use_global_device_ids=true, to_apply=%region_8.9 | all-reduce | flops 6 | bytes 48 | tf_op jit(solution)/shard_map/psum | solution.py:101
  252.6 91.8 %reduce-scatter.3.cloned.1.call-done = bf16[24,512]{1,0:T(8,128)(2,1)} async-done(((bf16[768,512]{1,0:T(8,128)(2,1)}), bf16[24,512]{1,0:T(8,128)(2,1)}) %reduce-scatter.3.cloned.1.call-update) | async-done | bytes 24592 | tf_op jit(solution)/shard_map/reduce_scatter | solution.py:94
  344.4 149.8 %reduce-scatter.5.cloned.1.call-done = bf16[24,512]{1,0:T(8,128)(2,1)} async-done(((bf16[768,512]{1,0:T(8,128)(2,1)}), bf16[24,512]{1,0:T(8,128)(2,1)}) %reduce-scatter.5.cloned.1.call-update) | async-done | bytes 24592 | tf_op jit(solution)/shard_map/reduce_scatter | solution.py:97
  (174 shorter events, 72.7 us)
Async XLA Ops:
  7.2 3.0 copy-start.5
  7.2 4.1 copy-start.7
  7.2 337.2 %reduce-scatter.3.cloned.1.call-start = ((), (), s32[]{:S(2)}) async-start(), calls=%async_computation.2 | async-start | bytes 811008 | tf_op jit(solution)/shard_map/reduce_scatter | solution.py:94
  105.2 2.9 copy-start.9
  108.1 4.2 copy-start.2
  118.6 2.5 copy-start
  121.1 1.9 copy-start.3
  123.0 4.2 copy-start.2
  133.5 2.5 copy-start
  136.0 1.9 copy-start.3
  137.9 4.2 copy-start.2
  148.4 2.5 copy-start
  151.0 1.9 copy-start.3
  152.9 4.2 copy-start.2
  163.3 2.5 copy-start
  165.9 1.9 copy-start.3
  167.8 4.2 copy-start.2
  178.2 2.5 copy-start
  180.8 1.9 copy-start.3
  182.7 4.2 copy-start.2
  193.2 2.5 copy-start
  195.7 1.9 copy-start.3
  200.2 293.9 %reduce-scatter.5.cloned.1.call-start = ((), (), s32[]{:S(2)}) async-start(), calls=%async_computation.3 | async-start | bytes 811008 | tf_op jit(solution)/shard_map/reduce_scatter | solution.py:97
  200.3 50.8 %copy-start.6 = (bf16[6,768,64]{1,2,0:T(8,128)(2,1)S(1)}, bf16[6,768,64]{1,2,0:T(8,128)(2,1)}, u32[]{:S(2)}) copy-start(bf16[6,768,64]{1,2,0:T(8,128)(2,1)} %get-tuple-element.64) | copy-start | bytes 1769476
  (13 other events, 14.1 us)
Sparse Core Ops, SparseCore 0:
  200.3 144.0 reduce-scatter.2
  348.0 146.1 reduce-scatter.4
where the time goes:
time: 506 us; the launch traced here: 501 us
  waiting for transfers between devices  242 us (48%)
  blocking collectives  142 us (28%)
  matrix products  50 us (10%)
  local copies, waits for them, and re-layouts  42.1 us (8%)
  between operations  14.1 us (3%)
  other arithmetic  10.3 us (2%)
    reduce_scatter x1, waiting for transfers between devices, local(): lax.psum_scatter(parts[1].astype(jnp.bfloat16), 'head', scatter_dimension...  150 us
    reduce_scatter x1, waiting for transfers between devices, local(): lax.psum_scatter(parts[0].astype(jnp.bfloat16), 'head', scatter_dimension...  91.8 us
    psum x1, blocking collectives, local(): gate_grad = lax.psum(gate_terms, 'dp') / lax.axis_size('dp')  49.6 us
    all_gather x1, blocking collectives, local(): lax.all_gather(key_rows[0], 'head', axis=0, tiled=True)  49 us
    all_gather x1, blocking collectives, local(): lax.all_gather(value_rows[0], 'head', axis=0, tiled=True)  43.9 us
    dynamic_slice x24, local copies, waits for them, and re-layouts, local(): lax.scan(head_step, (zero_sums, zero_sums), (q_heads, k_heads, v_heads, d...  15.8 us
    while x60, local copies, waits for them, and re-layouts  11 us
  transfers between devices with their start and end apart: 2, of which 2 were waited for; matrix products, arithmetic and copies ran while one was open for 1% of the time, Pallas kernels for 0%

commit v1 on v0

v1 whole, which is shorter than its diff:
```python
import functools

import jax
import jax.numpy as jnp
from jax import lax
from jax.experimental import pallas as pl
from jax.experimental.pallas import tpu as pltpu
from jax.sharding import PartitionSpec as P

HEAD_DIM = 64
KV_HEADS = 8
GROUP_HEADS = 29
SEQ = 768
HEADS = 6
PAIRS = 3
BLK = 256
NBLK = SEQ // BLK
KV_COLS = KV_HEADS * HEAD_DIM
Q_COLS = HEADS * HEAD_DIM
OWN = 24
CHIP = 48
XROWS = 192
SCALE = 0.125
SCALE_LOG2 = 0.125 * 1.4426950408889634
NEG = -1e30
MESH = pl.DeviceIdType.MESH
F32 = jnp.float32
BF16 = jnp.bfloat16


def dot(a, b):
    return lax.dot_general(a, b, (((1,), (0,)), ((), ())), preferred_element_type=F32)


def dot_t(a, b):
    return lax.dot_general(a, b, (((1,), (1,)), ((), ())), preferred_element_type=F32)


def fold(values, op):
    rows, cols = values.shape
    return op(values.reshape(rows // 8, 8, cols), axis=0)


def pack_rows(k, v):
    return jnp.concatenate([k[0:16], v[0:16], k[16:24], v[16:24]], axis=0)


def unpack_rows(block):
    k = jnp.concatenate([block[0:16], block[32:40]], axis=0)
    v = jnp.concatenate([block[16:32], block[40:48]], axis=0)
    return k, v


def kernel(
    slots, gates, q_hbm, dy_hbm, key_ref, value_ref,
    dq_hbm, dk_ref, dv_ref, gg_ref,
    shards, k_all, v_all, sel_t, k_sel, v_sel, k_sel_t, q_ref, dy_ref, dyg_ref, dq_ref,
    s_ref, dp_ref, p_ref, ds_ref, gate_acc, gate_recv,
    part, part_recv, chip_sum, x_recv, x_sum, z_recv,
    load_sem, store_sem, ag_recv, ag_z, ag_x, ag_c,
    c_send, c_recv, x_send, x_recv_sem, z_send, z_recv_sem, g_send, g_recv,
):
    me = lax.axis_index("head")
    x, z, c = me // 8, (me // 2) % 4, me % 2
    dp = lax.axis_index("dp")
    y, zh = dp // 4, dp % 4

    def head_id(xx, zz, cc):
        return {"head": (xx * 4 + zz) * 2 + cc}

    def dp_id(yy, hh):
        return {"dp": yy * 4 + hh}

    partners = (
        [head_id((x + d) % 4, z, c) for d in (1, 2, 3)]
        + [head_id(x, (z + d) % 4, c) for d in (1, 2, 3)]
        + [head_id(x, z, 1 - c)]
        + [dp_id((y + d) % 4, zh) for d in (1, 2, 3)]
        + [dp_id(y, (zh + d) % 4) for d in (1, 2, 3)]
    )
    barrier = pltpu.get_barrier_semaphore()
    for partner in partners:
        pl.semaphore_signal(barrier, inc=1, device_id=partner, device_id_type=MESH)

    loads = []
    for p in range(PAIRS):
        cols = pl.ds(p * 128, 128)
        loads.append(pltpu.make_async_copy(q_hbm.at[0, :, cols], q_ref.at[p], load_sem.at[0, p]))
        loads.append(pltpu.make_async_copy(dy_hbm.at[0, :, cols], dy_ref.at[p], load_sem.at[1, p]))
    for load in loads:
        load.start()

    shards[x, z, c] = pack_rows(
        key_ref[0].astype(F32), value_ref[0].astype(F32)
    ).astype(BF16)

    pl.semaphore_wait(barrier, len(partners))

    def shard_copy(xx, zz, cc, send_sem, target):
        return pltpu.make_async_remote_copy(
            src_ref=shards.at[xx, zz, cc], dst_ref=shards.at[xx, zz, cc],
            send_sem=send_sem, recv_sem=ag_recv.at[xx, zz, cc],
            device_id=target, device_id_type=MESH,
        )

    sends = []

    def send(copy):
        copy.start()
        sends.append(copy)

    def arrived(xx, zz, cc):
        shard_copy(xx, zz, cc, ag_z.at[0], head_id(x, z, 1 - c)).wait_recv()

    for d in (1, 2, 3):
        send(shard_copy(x, z, c, ag_z.at[d - 1], head_id(x, (z + d) % 4, c)))
    for dz in range(4):
        zz = (z + dz) % 4
        if dz:
            arrived(x, zz, c)
        for d in (1, 3, 2):
            send(shard_copy(x, zz, c, ag_x.at[dz, d - 1], head_id((x + d) % 4, z, c)))
        send(shard_copy(x, zz, c, ag_c.at[0, dz], head_id(x, z, 1 - c)))
    for d in (1, 3, 2):
        for dz in range(4):
            xx, zz = (x + d) % 4, (z + dz) % 4
            arrived(xx, zz, c)
            send(shard_copy(xx, zz, c, ag_c.at[d, dz], head_id(x, z, 1 - c)))

    row = lax.broadcasted_iota(jnp.int32, (Q_COLS, KV_COLS), 0)
    col = lax.broadcasted_iota(jnp.int32, (Q_COLS, KV_COLS), 1)
    slot_of_row = row // HEAD_DIM
    group_of_row = jnp.zeros((Q_COLS, KV_COLS), jnp.int32)
    for h in range(HEADS):
        group_of_row = jnp.where(slot_of_row == h, slots[h] // GROUP_HEADS, group_of_row)
    wanted = group_of_row * HEAD_DIM + row % HEAD_DIM
    sel_t[...] = jnp.where(col == wanted, 1.0, 0.0).astype(BF16)

    for load in loads:
        load.wait()
    lane = lax.broadcasted_iota(jnp.int32, (1, 128), 1)
    low_half = lane < HEAD_DIM
    for p in range(PAIRS):
        gate = jnp.where(low_half, gates[2 * p], gates[2 * p + 1])
        dyg_ref[p] = (dy_ref[p].astype(F32) * gate).astype(BF16)

    def unpack_x(xx):
        for zz in range(4):
            rows = pl.ds(XROWS * xx + CHIP * zz, CHIP)
            k0, v0 = unpack_rows(shards[xx, zz, 0].astype(F32))
            k1, v1 = unpack_rows(shards[xx, zz, 1].astype(F32))
            k_all[rows, :] = jnp.concatenate([k0, k1], axis=0).astype(BF16)
            v_all[rows, :] = jnp.concatenate([v0, v1], axis=0).astype(BF16)

    def select_block(j):
        rows = pl.ds(BLK * j, BLK)
        keys, values, chosen = k_all[rows, :], v_all[rows, :], sel_t[...]
        k_block = dot_t(keys, chosen).astype(BF16)
        v_block = dot_t(values, chosen).astype(BF16)
        for p in range(PAIRS):
            k_sel[p, rows, :] = k_block[:, p * 128 : (p + 1) * 128]
            v_sel[p, rows, :] = v_block[:, p * 128 : (p + 1) * 128]
        k_t = dot_t(chosen, keys).astype(BF16)
        for p in range(PAIRS):
            k_sel_t[p, :, rows] = k_t[p * 128 : (p + 1) * 128, :]

    key_pos = lax.broadcasted_iota(jnp.int32, (BLK, BLK), 0)
    query_pos = lax.broadcasted_iota(jnp.int32, (BLK, BLK), 1)
    causal = key_pos <= query_pos
    half_masks = (low_half, jnp.logical_not(low_half))

    def forward_block(i):
        queries = pl.ds(BLK * i, BLK)

        def pair_step(p, carry):
            dq_t = []
            for half in range(2):
                mask = half_masks[half]
                h = 2 * p + half
                q_half = jnp.where(mask, q_ref[p, queries, :], jnp.zeros((), BF16))
                dy_half = jnp.where(mask, dyg_ref[p, queries, :], jnp.zeros((), BF16))
                top = jnp.full((8, BLK), NEG, F32)
                for j in range(i + 1):
                    keys = pl.ds(BLK * j, BLK)
                    s = dot_t(k_sel[p, keys, :], q_half)
                    if j == i:
                        s = jnp.where(causal, s, NEG)
                    top = jnp.maximum(top, fold(s, jnp.max))
                    s_ref[half, keys, :] = s
                    dp_ref[half, keys, :] = dot_t(v_sel[p, keys, :], dy_half)
                top = jnp.max(top, axis=0, keepdims=True) * SCALE_LOG2
                total = jnp.zeros((8, BLK), F32)
                weighted = jnp.zeros((8, BLK), F32)
                step = 64
                for k0 in range(0, BLK * (i + 1), step):
                    keys = pl.ds(k0, step)
                    e = jnp.exp2(s_ref[half, keys, :] * SCALE_LOG2 - top)
                    s_ref[half, keys, :] = e
                    total = total + fold(e, jnp.sum)
                    weighted = weighted + fold(e * dp_ref[half, keys, :], jnp.sum)
                inverse = 1.0 / jnp.sum(total, axis=0, keepdims=True)
                delta = jnp.sum(weighted, axis=0, keepdims=True) * inverse
                for k0 in range(0, BLK * (i + 1), step):
                    keys = pl.ds(k0, step)
                    w = s_ref[half, keys, :] * inverse
                    p_ref[h, keys, queries] = w.astype(BF16)
                    ds_ref[h, keys, queries] = (w * (dp_ref[half, keys, :] - delta)).astype(BF16)
                depth = BLK * (i + 1)
                dq_t.append(
                    SCALE * dot(
                        k_sel_t[p, half * 64 : (half + 1) * 64, 0:depth],
                        ds_ref[h, 0:depth, queries],
                    )
                )
                gate_fold = delta[:, 0:128] + delta[:, 128:256]
                if i == 0:
                    gate_acc[0, pl.ds(h, 1), :] = gate_fold
                else:
                    gate_acc[0, pl.ds(h, 1), :] = gate_acc[0, pl.ds(h, 1), :] + gate_fold
            dq_ref[p, queries, :] = jnp.concatenate(dq_t, axis=0).T.astype(BF16)
            return carry

        lax.fori_loop(0, PAIRS, pair_step, 0)

    stores = []

    def store_queries(i):
        for p in range(PAIRS):
            copy = pltpu.make_async_copy(
                dq_ref.at[p, pl.ds(BLK * i, BLK), :],
                dq_hbm.at[0, pl.ds(BLK * i, BLK), pl.ds(128 * p, 128)],
                store_sem.at[i, p],
            )
            copy.start()
            stores.append(copy)

    gate_acc[0] = jnp.zeros((8, 128), F32)
    ready = ((0, 1), (2,), (3,))
    for i in range(NBLK):
        for xx in ready[i]:
            for zz in range(4):
                arrived(xx, zz, 1 - c)
            unpack_x(xx)
        select_block(i)
        forward_block(i)
        store_queries(i)

    def gate_copy(stage, d, target):
        return pltpu.make_async_remote_copy(
            src_ref=gate_acc.at[stage], dst_ref=gate_recv.at[stage, d - 1],
            send_sem=g_send.at[stage, d - 1], recv_sem=g_recv.at[stage, d - 1],
            device_id=target, device_id_type=MESH,
        )

    for d in (1, 2, 3):
        send(gate_copy(0, d, dp_id((y + d) % 4, zh)))

    def split(lo, hi):
        cuts = sorted({lo, hi} | {b for b in range(0, SEQ, BLK) if lo < b < hi})
        return list(zip(cuts[:-1], cuts[1:]))

    def head_grads(weights_ref, other_ref, lo, hi):
        pieces = []
        for a, b in split(lo, hi):
            start = (a // BLK) * BLK
            row_parts = []
            for p in range(PAIRS):
                even = dot(weights_ref[2 * p, a:b, start:SEQ], other_ref[p, start:SEQ, :])
                odd = dot(weights_ref[2 * p + 1, a:b, start:SEQ], other_ref[p, start:SEQ, :])
                row_parts.append(jnp.where(low_half, even, odd))
            pieces.append(jnp.concatenate(row_parts, axis=1))
        return jnp.concatenate(pieces, axis=0)

    def chip_copy(xx):
        return pltpu.make_async_remote_copy(
            src_ref=part.at[xx, 1 - c], dst_ref=part_recv.at[xx],
            send_sem=c_send.at[xx], recv_sem=c_recv.at[xx],
            device_id=head_id(x, z, 1 - c), device_id_type=MESH,
        )

    def x_copy(xx):
        return pltpu.make_async_remote_copy(
            src_ref=chip_sum.at[xx], dst_ref=x_recv.at[x],
            send_sem=x_send.at[xx], recv_sem=x_recv_sem.at[x],
            device_id=head_id(xx, z, c), device_id_type=MESH,
        )

    def key_block(xx):
        lo, hi = XROWS * xx, XROWS * (xx + 1)
        dk = (SCALE * head_grads(ds_ref, q_ref, lo, hi)).astype(BF16)
        dv = head_grads(p_ref, dyg_ref, lo, hi).astype(BF16)
        dk = dot(dk, sel_t[...])
        dv = dot(dv, sel_t[...])
        for zz in range(4):
            for cc in range(2):
                at = CHIP * zz + OWN * cc
                part[xx, cc, zz] = pack_rows(dk[at : at + OWN], dv[at : at + OWN]).astype(BF16)
        send(chip_copy(xx))

    def chip_add(xx):
        chip_copy(xx).wait_recv()
        for zz in range(4):
            chip_sum[xx, zz] = (
                part[xx, c, zz].astype(F32) + part_recv[xx, zz].astype(F32)
            ).astype(BF16)

        @pl.when(xx != x)
        def _():
            x_copy(xx).start()

    for xx in range(4):
        key_block(xx)
        if xx:
            chip_add(xx - 1)
    chip_add(3)

    gate_sum = gate_acc[0]
    for d in (1, 2, 3):
        gate_copy(0, d, dp_id(y, zh)).wait_recv()
        gate_sum = gate_sum + gate_recv[0, d - 1]
    gate_acc[1] = gate_sum
    for d in (1, 2, 3):
        send(gate_copy(1, d, dp_id(y, (zh + d) % 4)))

    for d in (1, 3, 2):
        src = (x + d) % 4
        pltpu.make_async_remote_copy(
            src_ref=chip_sum.at[src], dst_ref=x_recv.at[src],
            send_sem=x_send.at[src], recv_sem=x_recv_sem.at[src],
            device_id=head_id(src, z, c), device_id_type=MESH,
        ).wait_recv()

    def z_copy(d):
        zz = (z + d) % 4
        return pltpu.make_async_remote_copy(
            src_ref=x_sum.at[zz], dst_ref=z_recv.at[d - 1],
            send_sem=z_send.at[d - 1], recv_sem=z_recv_sem.at[d - 1],
            device_id=head_id(x, zz, c), device_id_type=MESH,
        )

    own = None
    for d in (1, 2, 3, 0):
        zz = (z + d) % 4
        total = chip_sum[x, zz].astype(F32)
        for dx in (1, 2, 3):
            total = total + x_recv[(x + dx) % 4, zz].astype(F32)
        if d:
            x_sum[zz] = total.astype(BF16)
            send(z_copy(d))
        else:
            own = total
    gate_sum = gate_acc[1]
    for d in (1, 2, 3):
        gate_copy(1, d, dp_id(y, zh)).wait_recv()
        gate_sum = gate_sum + gate_recv[1, d - 1]
    for h in range(HEADS):
        gg_ref[h] = jnp.sum(gate_sum[h : h + 1, :]) / (16.0 * gates[h])
    for d in (1, 2, 3):
        z_copy(d).wait_recv()
        own = own + z_recv[d - 1].astype(F32)
    dk, dv = unpack_rows(own)
    dk_ref[0] = dk.astype(BF16)
    dv_ref[0] = dv.astype(BF16)

    for d in (1, 2, 3):
        x_copy((x + d) % 4).wait_send()
    for copy in sends:
        copy.wait_send()
    for copy in stores:
        copy.wait()


def local(queries, key_rows, value_rows, upstream, head_gate, slot_heads):
    vmem = pl.BlockSpec(memory_space=pltpu.VMEM)
    smem = pl.BlockSpec(memory_space=pltpu.SMEM)
    hbm = pl.BlockSpec(memory_space=pl.ANY)
    dma = pltpu.SemaphoreType.DMA
    return pl.pallas_call(
        kernel,
        out_shape=(
            jax.ShapeDtypeStruct(queries.shape, BF16),
            jax.ShapeDtypeStruct(key_rows.shape, BF16),
            jax.ShapeDtypeStruct(value_rows.shape, BF16),
            jax.ShapeDtypeStruct(head_gate.shape, F32),
        ),
        in_specs=[smem, smem, hbm, hbm, vmem, vmem],
        out_specs=(hbm, vmem, vmem, smem),
        scratch_shapes=[
            pltpu.VMEM((4, 4, 2, CHIP, KV_COLS), BF16),
            pltpu.VMEM((SEQ, KV_COLS), BF16),
            pltpu.VMEM((SEQ, KV_COLS), BF16),
            pltpu.VMEM((Q_COLS, KV_COLS), BF16),
            pltpu.VMEM((PAIRS, SEQ, 128), BF16),
            pltpu.VMEM((PAIRS, SEQ, 128), BF16),
            pltpu.VMEM((PAIRS, 128, SEQ), BF16),
            pltpu.VMEM((PAIRS, SEQ, 128), BF16),
            pltpu.VMEM((PAIRS, SEQ, 128), BF16),
            pltpu.VMEM((PAIRS, SEQ, 128), BF16),
            pltpu.VMEM((PAIRS, SEQ, 128), BF16),
            pltpu.VMEM((2, SEQ, BLK), F32),
            pltpu.VMEM((2, SEQ, BLK), F32),
            pltpu.VMEM((HEADS, SEQ, SEQ), BF16),
            pltpu.VMEM((HEADS, SEQ, SEQ), BF16),
            pltpu.VMEM((2, 8, 128), F32),
            pltpu.VMEM((2, 3, 8, 128), F32),
            pltpu.VMEM((4, 2, 4, CHIP, KV_COLS), BF16),
            pltpu.VMEM((4, 4, CHIP, KV_COLS), BF16),
            pltpu.VMEM((4, 4, CHIP, KV_COLS), BF16),
            pltpu.VMEM((4, 4, CHIP, KV_COLS), BF16),
            pltpu.VMEM((4, CHIP, KV_COLS), BF16),
            pltpu.VMEM((3, CHIP, KV_COLS), BF16),
            dma((2, PAIRS)), dma((NBLK, PAIRS)),
            dma((4, 4, 2)), dma((3,)), dma((4, 3)), dma((4, 4)),
            dma((4,)), dma((4,)), dma((4,)), dma((4,)), dma((3,)), dma((3,)),
            dma((2, 3)), dma((2, 3)),
        ],
        compiler_params=pltpu.CompilerParams(
            collective_id=0, has_side_effects=True, vmem_limit_bytes=56 * 1024 * 1024
        ),
        name="attention_backward",
    )(slot_heads, head_gate, queries, upstream, key_rows, value_rows)


def solution(mesh):
    in_specs = (
        P("dp", None, "head"),
        P("dp", "head", None),
        P("dp", "head", None),
        P("dp", None, "head"),
        P("head"),
        P("head"),
    )
    out_specs = (P("dp", None, "head"), P("dp", "head", None), P("dp", "head", None), P("head"))
    return jax.shard_map(local, mesh=mesh, in_specs=in_specs, out_specs=out_specs, check_vma=False)
```

time: 506 us -> 70.3 us (0.14)
  waiting for transfers between devices: 242 us -> 0 us
  blocking collectives: 142 us -> 0 us
  Pallas kernels: 0 us -> 64.9 us
  matrix products: 50 us -> 0 us
  local copies, waits for them, and re-layouts: 42.1 us -> 3.84 us
  between operations: 14.1 us -> 0.65 us
  other arithmetic: 10.3 us -> 0 us
    reduce_scatter x2 -> x0, waiting for transfers between devices: 242 us -> none  [the longest x1 150 us: local(): lax.psum_scatter(parts[1].astype(jnp.bfloat16), 'head', scatter_dimension...]
    all_gather x2 -> x0, blocking collectives: 92.9 us -> none  [the longest x1 49 us: local(): lax.all_gather(key_rows[0], 'head', axis=0, tiled=True)]
    pallas_call x0 -> x1, Pallas kernels: none -> 64.9 us  [local(): pl.pallas_call(kernel, out_shape=(jax.ShapeDtypeStruct(queries.shape, BF1...]
    dot_general x38 -> x0, matrix products: 50 us -> none  [the longest x6 9.82 us: query_side(): attended = jnp.dot(weights_low, v_head, preferred_element_type=jnp.float32)]
    psum x1 -> x0, blocking collectives: 49.6 us -> none  [local(): gate_grad = lax.psum(gate_terms, 'dp') / lax.axis_size('dp')]
    dynamic_slice x24 -> x0, local copies, waits for them, and re-layouts: 15.8 us -> none  [local(): lax.scan(head_step, (zero_sums, zero_sums), (q_heads, k_heads, v_heads, d...]
    while x62 -> x0, local copies, waits for them, and re-layouts: 14.7 us -> none
  transfers between devices with their start and end apart: 2 -> 0, of which waited for: 2 -> 0; matrix products, arithmetic and copies ran while one was open for 1% -> 0% of each run, Pallas kernels for 0% -> 0%
where the time goes in v1:
time: 70.3 us; the launch traced here: 69.3 us
  Pallas kernels  64.9 us (92%)
  local copies, waits for them, and re-layouts  3.84 us (5%)
    pallas_call x1, Pallas kernels, local(): pl.pallas_call(kernel, out_shape=(jax.ShapeDtypeStruct(queries.shape, BF1...  64.9 us
    unnamed x10, local copies, waits for them, and re-layouts  3.84 us

profile of v1, /device:TPU:1, one launch (start us, length us, event | category | flops | bytes accessed | tf_op | source)
XLA Modules:
  0.0 69.3 jit_solution(12219672396427731735)
XLA Ops:
  0.6 64.9 %attention_backward.1 = (bf16[1,768,384]{2,1,0:T(8,128)(2,1)}, bf16[1,24,512]{2,1,0:T(8,128)(2,1)}, bf16[1,24,512]{2,1,0:T(8,128)(2,1)}, f32[6]{0:T(128)}) custom-call(s32[6]{0:T(128)} %slots.1, f32[6]{0:T(128)} %gates.1, bf16[1,768,384]{2,1,0:T(8,128)(2,1)} %q_hbm.1, bf16[1,768,384]{2,1,0:T(8,128)(2,1)} %dy_hbm.1, bf16[1,24,512]{2,1,0:T(8,128)(2,1)} %key_ref.1, ...), custom_call_target="tpu_custom_call" | custom-call | tf_op jit(solution)/shard_map/attention_backward/pallas_call | solution.py:378
  65.5 0.0 copy-start.1
  65.5 1.9 %copy.14 = bf16[1,768,384]{2,1,0:T(8,128)(2,1)} copy(bf16[1,768,384]{2,1,0:T(8,128)(2,1)} %get-tuple-element.8) | data formatting | bytes 1179648
  67.4 0.0 copy-done.1
  67.5 0.0 copy-start
  67.5 0.6 copy.15
  68.1 0.1 copy-done
  68.2 0.0 copy-start.2
  68.2 0.6 copy.16
  68.8 0.0 copy-done.2
  68.8 0.5 copy.17
Async XLA Ops:
  65.5 2.0 %copy-start.1 = (bf16[1,24,512]{2,1,0:T(8,128)(2,1)S(1)}, bf16[1,24,512]{2,1,0:T(8,128)(2,1)}, u32[]{:S(2)}) copy-start(bf16[1,24,512]{2,1,0:T(8,128)(2,1)} %get-tuple-element.9) | copy-start | bytes 73732
  67.5 0.7 %copy-start = (bf16[1,24,512]{2,1,0:T(8,128)(2,1)S(1)}, bf16[1,24,512]{2,1,0:T(8,128)(2,1)}, u32[]{:S(2)}) copy-start(bf16[1,24,512]{2,1,0:T(8,128)(2,1)} %get-tuple-element.10) | copy-start | bytes 73732
  68.2 0.6 copy-start.2

commit v2 on v1

v2 whole, which is shorter than its diff:
```python
import functools

import jax
import jax.numpy as jnp
from jax import lax
from jax.experimental import pallas as pl
from jax.experimental.pallas import tpu as pltpu
from jax.sharding import PartitionSpec as P

HEAD_DIM = 64
KV_HEADS = 8
GROUP_HEADS = 29
SEQ = 768
HEADS = 6
PAIRS = 3
BLK = 256
NBLK = SEQ // BLK
KV_COLS = KV_HEADS * HEAD_DIM
Q_COLS = HEADS * HEAD_DIM
OWN = 24
CHIP = 48
XROWS = 192
SCALE = 0.125
SCALE_LOG2 = 0.125 * 1.4426950408889634
NEG = -1e30
MESH = pl.DeviceIdType.MESH
F32 = jnp.float32
BF16 = jnp.bfloat16


def dot(a, b):
    return lax.dot_general(a, b, (((1,), (0,)), ((), ())), preferred_element_type=F32)


def dot_t(a, b):
    return lax.dot_general(a, b, (((1,), (1,)), ((), ())), preferred_element_type=F32)


def fold(values, op):
    rows, cols = values.shape
    return op(values.reshape(rows // 8, 8, cols), axis=0)


def pack_rows(rows):
    return jnp.concatenate([rows[:, : KV_COLS // 2], rows[:, KV_COLS // 2 :]], axis=0)


def unpack_rows(block):
    return jnp.concatenate([block[0:OWN], block[OWN:CHIP]], axis=1)


KEY, VALUE = 0, 1


def kernel(
    slots, gates, q_hbm, dy_hbm, key_ref, value_ref,
    dq_hbm, dk_ref, dv_ref, gg_ref,
    shards, k_all, sel_t, k_sel, v_sel, k_sel_t, q_ref, dy_ref, dyg_ref, qn_ref, dyn_ref, dq_ref,
    s_ref, p_ref, ds_ref, scale_ref, gate_acc, gate_recv,
    part, part_recv, chip_sum, x_recv, x_sum, z_recv,
    load_sem, store_sem, agz_send, agz_recv, agx_send, agx_recv, agc_send, agc_recv,
    c_send, c_recv, x_send, x_recv_sem, z_send, z_recv_sem, g_send, g_recv, go,
):
    me = lax.axis_index("head")
    x, z, c = me // 8, (me // 2) % 4, me % 2
    dp = lax.axis_index("dp")
    y, zh = dp // 4, dp % 4

    def head_id(xx, zz, cc):
        return {"head": (xx * 4 + zz) * 2 + cc}

    def dp_id(yy, hh):
        return {"dp": yy * 4 + hh}

    sibling = head_id(x, z, 1 - c)
    near = (z + 1 - 2 * (z % 2), 2 - z // 2, 3 - 3 * (z // 2))

    barrier = pltpu.get_barrier_semaphore()

    def greet(target):
        pl.semaphore_signal(barrier, inc=1, device_id=target, device_id_type=MESH)

    for d in (1, 2, 3):
        greet(head_id(x, (z + d) % 4, c))
        greet(head_id((x + d) % 4, z, c))
        greet(dp_id((y + d) % 4, zh))
    greet(sibling)
    for d in (1, 2, 3):
        pl.when((zh + d) % 4 > zh)(lambda d=d: greet(dp_id(y, (zh + d) % 4)))

    loads = []
    for p in range(PAIRS):
        cols = pl.ds(p * 128, 128)
        loads.append(pltpu.make_async_copy(q_hbm.at[0, :, cols], q_ref.at[p], load_sem.at[0, p]))
        loads.append(pltpu.make_async_copy(dy_hbm.at[0, :, cols], dy_ref.at[p], load_sem.at[1, p]))
    for load in loads:
        load.start()

    shards[KEY, x, c, z] = pack_rows(key_ref[0].astype(F32)).astype(BF16)
    shards[VALUE, x, c, z] = pack_rows(value_ref[0].astype(F32)).astype(BF16)

    pl.semaphore_wait(barrier, 10 + zh)

    sends = []

    def send(copy):
        copy.start()
        sends.append(copy)

    def z_shard(t, source, slot, target):
        return pltpu.make_async_remote_copy(
            src_ref=shards.at[t, x, c, source], dst_ref=shards.at[t, x, c, source],
            send_sem=agz_send.at[t, slot], recv_sem=agz_recv.at[t, source],
            device_id=target, device_id_type=MESH,
        )

    def x_shard(t, xx, zz, slot, d, target):
        return pltpu.make_async_remote_copy(
            src_ref=shards.at[t, xx, c, zz], dst_ref=shards.at[t, xx, c, zz],
            send_sem=agx_send.at[t, slot, d - 1], recv_sem=agx_recv.at[t, xx, zz],
            device_id=target, device_id_type=MESH,
        )

    def c_block(t, xx, cc):
        return pltpu.make_async_remote_copy(
            src_ref=shards.at[t, xx, cc], dst_ref=shards.at[t, xx, cc],
            send_sem=agc_send.at[t, xx], recv_sem=agc_recv.at[t, xx],
            device_id=sibling, device_id_type=MESH,
        )

    def send_z(t):
        for slot, zz in enumerate(near):
            send(z_shard(t, z, slot, head_id(x, zz, c)))

    def send_x(t, slot, zz):
        for d in (1, 3, 2):
            send(x_shard(t, x, zz, slot, d, head_id((x + d) % 4, z, c)))

    def forward_z(t):
        for slot, zz in enumerate(near):
            z_shard(t, zz, slot, sibling).wait_recv()
            send_x(t, slot + 1, zz)
        send(c_block(t, x, c))

    def forward_x(t):
        for d in (1, 3, 2):
            xx = (x + d) % 4
            for zz in (z,) + near:
                x_shard(t, xx, zz, 0, d, sibling).wait_recv()
            send(c_block(t, xx, c))

    send_z(KEY)
    send_x(KEY, 0, z)
    send_z(VALUE)
    forward_z(KEY)
    send_x(VALUE, 0, z)
    forward_z(VALUE)

    for d in (1, 2, 3):
        pl.when((zh + d) % 4 < zh)(
            lambda d=d: pl.semaphore_signal(
                go.at[3 - d], inc=1, device_id=dp_id(y, (zh + d) % 4), device_id_type=MESH
            )
        )

    row = lax.broadcasted_iota(jnp.int32, (Q_COLS, KV_COLS), 0)
    col = lax.broadcasted_iota(jnp.int32, (Q_COLS, KV_COLS), 1)
    slot_of_row = row // HEAD_DIM
    group_of_row = jnp.zeros((Q_COLS, KV_COLS), jnp.int32)
    for h in range(HEADS):
        group_of_row = jnp.where(slot_of_row == h, slots[h] // GROUP_HEADS, group_of_row)
    wanted = group_of_row * HEAD_DIM + row % HEAD_DIM
    sel_t[...] = jnp.where(col == wanted, 1.0, 0.0).astype(BF16)

    for load in loads:
        load.wait()
    low_half = lax.broadcasted_iota(jnp.int32, (1, 128), 1) < HEAD_DIM
    half_masks = (low_half, jnp.logical_not(low_half))
    for p in range(PAIRS):
        gate = jnp.where(low_half, gates[2 * p], gates[2 * p + 1])
        dyg_ref[p] = (dy_ref[p].astype(F32) * gate).astype(BF16)

    def select_x(t, xx):
        c_block(t, xx, 1 - c).wait_recv()
        blocks = []
        for zz in range(4):
            for cc in range(2):
                blocks.append(unpack_rows(shards[t, xx, cc, zz].astype(F32)))
        table = jnp.concatenate(blocks, axis=0).astype(BF16)
        rows = pl.ds(pl.multiple_of(XROWS * xx, XROWS), XROWS)
        if t == KEY:
            k_all[rows, :] = table
        chosen = dot_t(table, sel_t[...]).astype(BF16)
        target = k_sel if t == KEY else v_sel
        for p in range(PAIRS):
            target[p, rows, :] = chosen[:, p * 128 : (p + 1) * 128]

    forward_x(KEY)
    for d in (0, 1, 3, 2):
        select_x(KEY, (x + d) % 4)

    key_pos = lax.broadcasted_iota(jnp.int32, (BLK, BLK), 0)
    query_pos = lax.broadcasted_iota(jnp.int32, (BLK, BLK), 1)
    causal = key_pos <= query_pos
    STEP = 64

    def score_max(i, p, half):
        queries = pl.ds(BLK * i, BLK)
        q_half = jnp.where(half_masks[half], q_ref[p, queries, :], jnp.zeros((), BF16))
        top = jnp.full((8, BLK), NEG, F32)
        for j in range(i + 1):
            keys = pl.ds(BLK * j, BLK)
            s = dot_t(k_sel[p, keys, :], q_half)
            if j == i:
                s = jnp.where(causal, s, NEG)
            top = jnp.maximum(top, fold(s, jnp.max))
            s_ref[half, keys, :] = s
        return jnp.max(top, axis=0, keepdims=True) * SCALE_LOG2

    def exp_block(i, p, half, top):
        queries = pl.ds(BLK * i, BLK)
        h = 2 * p + half
        total = jnp.zeros((8, BLK), F32)
        for k0 in range(0, BLK * (i + 1), STEP):
            keys = pl.ds(k0, STEP)
            e = jnp.exp2(s_ref[half, keys, :] * SCALE_LOG2 - top)
            total = total + fold(e, jnp.sum)
            p_ref[h, keys, queries] = e.astype(BF16)
        inverse = 1.0 / jnp.sum(total, axis=0, keepdims=True)
        scale_ref[h, :, queries] = jnp.broadcast_to(inverse, (8, BLK))
        return jnp.broadcast_to(inverse, (HEAD_DIM, BLK))

    def score_block(i):
        queries = pl.ds(BLK * i, BLK)
        for p in range(PAIRS):
            tops = [score_max(i, p, half) for half in range(2)]
            scales = [exp_block(i, p, half, tops[half]) for half in range(2)]
            scale = jnp.concatenate(scales, axis=0).T
            dyn_ref[p, queries, :] = (dyg_ref[p, queries, :].astype(F32) * scale).astype(BF16)
            qn_ref[p, queries, :] = (q_ref[p, queries, :].astype(F32) * (scale * SCALE)).astype(BF16)

    def weight_grad(i, p, half):
        queries = pl.ds(BLK * i, BLK)
        h = 2 * p + half
        dy_half = jnp.where(half_masks[half], dyg_ref[p, queries, :], jnp.zeros((), BF16))
        weighted = jnp.zeros((8, BLK), F32)
        for j in range(i + 1):
            keys = pl.ds(BLK * j, BLK)
            dp = dot_t(v_sel[p, keys, :], dy_half)
            s_ref[half, keys, :] = dp
            weighted = weighted + fold(p_ref[h, keys, queries].astype(F32) * dp, jnp.sum)
        delta = jnp.sum(weighted, axis=0, keepdims=True) * scale_ref[h, 0:1, queries]
        gate_acc[0, h : h + 1, :] = (
            gate_acc[0, h : h + 1, :] + delta[:, 0:128] + delta[:, 128:256]
        )
        return delta

    def score_grad(i, p, half, delta):
        queries = pl.ds(BLK * i, BLK)
        h = 2 * p + half
        depth = BLK * (i + 1)
        for k0 in range(0, depth, STEP):
            keys = pl.ds(k0, STEP)
            ds_ref[h, keys, queries] = (
                p_ref[h, keys, queries].astype(F32) * (s_ref[half, keys, :] - delta)
            ).astype(BF16)

    def query_grad_t(i, p, half):
        queries = pl.ds(BLK * i, BLK)
        h = 2 * p + half
        depth = BLK * (i + 1)
        return (SCALE * scale_ref[h, 0:1, queries]) * dot(
            k_sel_t[p, half * 64 : (half + 1) * 64, 0:depth], ds_ref[h, 0:depth, queries]
        )

    def grad_block(i):
        queries = pl.ds(BLK * i, BLK)
        for p in range(PAIRS):
            deltas = [weight_grad(i, p, half) for half in range(2)]
            for half in range(2):
                score_grad(i, p, half, deltas[half])
            dq_t = [query_grad_t(i, p, half) for half in range(2)]
            dq_ref[p, queries, :] = jnp.concatenate(dq_t, axis=0).T.astype(BF16)

    stores = []

    def store_queries(i):
        for p in range(PAIRS):
            copy = pltpu.make_async_copy(
                dq_ref.at[p, pl.ds(BLK * i, BLK), :],
                dq_hbm.at[0, pl.ds(BLK * i, BLK), pl.ds(128 * p, 128)],
                store_sem.at[i, p],
            )
            copy.start()
            stores.append(copy)

    def split(lo, hi):
        cuts = sorted({lo, hi} | {b for b in range(0, SEQ, BLK) if lo < b < hi})
        return list(zip(cuts[:-1], cuts[1:]))

    def head_grads(weights_ref, other_ref, lo, hi):
        pieces = []
        for a, b in split(lo, hi):
            start = (a // BLK) * BLK
            row_parts = []
            for p in range(PAIRS):
                even = dot(weights_ref[2 * p, a:b, start:SEQ], other_ref[p, start:SEQ, :])
                odd = dot(weights_ref[2 * p + 1, a:b, start:SEQ], other_ref[p, start:SEQ, :])
                row_parts.append(jnp.where(low_half, even, odd))
            pieces.append(jnp.concatenate(row_parts, axis=1))
        return jnp.concatenate(pieces, axis=0)

    def chip_copy(t, xx):
        return pltpu.make_async_remote_copy(
            src_ref=part.at[t, xx, 1 - c], dst_ref=part_recv.at[t, xx],
            send_sem=c_send.at[t, xx], recv_sem=c_recv.at[t, xx],
            device_id=sibling, device_id_type=MESH,
        )

    def x_copy(t, xx):
        return pltpu.make_async_remote_copy(
            src_ref=chip_sum.at[t, xx], dst_ref=x_recv.at[t, x],
            send_sem=x_send.at[t, xx], recv_sem=x_recv_sem.at[t, x],
            device_id=head_id(xx, z, c), device_id_type=MESH,
        )

    def z_copy(t, slot, zz):
        return pltpu.make_async_remote_copy(
            src_ref=x_sum.at[t, zz], dst_ref=z_recv.at[t, z],
            send_sem=z_send.at[t, slot], recv_sem=z_recv_sem.at[t, z],
            device_id=head_id(x, zz, c), device_id_type=MESH,
        )

    def key_block(t, xx):
        lo, hi = XROWS * xx, XROWS * (xx + 1)
        if t == KEY:
            grads = head_grads(ds_ref, qn_ref, lo, hi)
        else:
            grads = head_grads(p_ref, dyn_ref, lo, hi)
        grads = dot(grads.astype(BF16), sel_t[...])
        for zz in range(4):
            for cc in range(2):
                at = CHIP * zz + OWN * cc
                part[t, xx, cc, zz] = pack_rows(grads[at : at + OWN]).astype(BF16)
        send(chip_copy(t, xx))

    def chip_add(t, xx):
        chip_copy(t, xx).wait_recv()
        for zz in range(4):
            chip_sum[t, xx, zz] = (
                part[t, xx, c, zz].astype(F32) + part_recv[t, xx, zz].astype(F32)
            ).astype(BF16)

        @pl.when(xx != x)
        def _():
            x_copy(t, xx).start()

    def x_add(t):
        for d in (1, 3, 2):
            src = (x + d) % 4
            pltpu.make_async_remote_copy(
                src_ref=chip_sum.at[t, src], dst_ref=x_recv.at[t, src],
                send_sem=x_send.at[t, src], recv_sem=x_recv_sem.at[t, src],
                device_id=head_id(src, z, c), device_id_type=MESH,
            ).wait_recv()
        for slot, zz in enumerate(near + (z,)):
            total = chip_sum[t, x, zz].astype(F32)
            for dx in (1, 2, 3):
                total = total + x_recv[t, (x + dx) % 4, zz].astype(F32)
            x_sum[t, zz] = total.astype(BF16)
            if slot < 3:
                send(z_copy(t, slot, zz))

    def z_add(t, out_ref):
        total = x_sum[t, z].astype(F32)
        for slot, zz in enumerate(near):
            pltpu.make_async_remote_copy(
                src_ref=x_sum.at[t, zz], dst_ref=z_recv.at[t, zz],
                send_sem=z_send.at[t, slot], recv_sem=z_recv_sem.at[t, zz],
                device_id=head_id(x, zz, c), device_id_type=MESH,
            ).wait_recv()
            total = total + z_recv[t, zz].astype(F32)
        out_ref[0] = unpack_rows(total).astype(BF16)

    def gate_copy(stage, d, target):
        return pltpu.make_async_remote_copy(
            src_ref=gate_acc.at[stage], dst_ref=gate_recv.at[stage, d - 1],
            send_sem=g_send.at[stage, d - 1], recv_sem=g_recv.at[stage, d - 1],
            device_id=target, device_id_type=MESH,
        )

    def gate_add(stage):
        total = gate_acc[stage]
        for d in (1, 2, 3):
            gate_copy(stage, d, sibling).wait_recv()
            total = total + gate_recv[stage, d - 1]
        return total

    gate_acc[0] = jnp.zeros((8, 128), F32)

    score_block(2)
    key_block(VALUE, 3)
    score_block(1)
    chip_add(VALUE, 3)
    key_block(VALUE, 2)
    forward_x(VALUE)
    score_block(0)
    chip_add(VALUE, 2)
    key_block(VALUE, 1)
    key_block(VALUE, 0)

    k_sel_t_all = dot_t(sel_t[...], k_all[...]).astype(BF16)
    for p in range(PAIRS):
        k_sel_t[p] = k_sel_t_all[p * 128 : (p + 1) * 128, :]
    for d in (0, 1, 3, 2):
        select_x(VALUE, (x + d) % 4)
    chip_add(VALUE, 1)
    chip_add(VALUE, 0)

    grad_block(2)
    key_block(KEY, 3)
    store_queries(2)
    grad_block(1)
    chip_add(KEY, 3)
    key_block(KEY, 2)
    store_queries(1)
    grad_block(0)
    for d in (1, 2, 3):
        send(gate_copy(0, d, dp_id((y + d) % 4, zh)))
    chip_add(KEY, 2)
    key_block(KEY, 1)
    store_queries(0)
    key_block(KEY, 0)
    chip_add(KEY, 1)
    gate_acc[1] = gate_add(0)
    for d in (1, 2, 3):
        pl.when((zh + d) % 4 > zh)(lambda d=d: pl.semaphore_wait(go.at[d - 1], 1))
    for d in (1, 2, 3):
        send(gate_copy(1, d, dp_id(y, (zh + d) % 4)))
    chip_add(KEY, 0)
    x_add(VALUE)
    z_add(VALUE, dv_ref)
    x_add(KEY)
    z_add(KEY, dk_ref)
    gate_sum = gate_add(1)
    for h in range(HEADS):
        gg_ref[h] = jnp.sum(gate_sum[h : h + 1, :]) / (16.0 * gates[h])

    for t in (KEY, VALUE):
        for d in (1, 2, 3):
            x_copy(t, (x + d) % 4).wait_send()
    for copy in sends:
        copy.wait_send()
    for copy in stores:
        copy.wait()


def finish(*refs):
    ins, outs, held = refs[:4], refs[4:8], refs[8:12]
    sem_in, sem_out = refs[12:]
    parts = [(n, pl.ds(BLK * k, BLK)) for k, n in enumerate((0, 0, 0))] + [(1, None), (2, None), (3, None)]

    def view(ref, rows):
        return ref if rows is None else ref.at[0, rows, :]

    fetch, store = [], []
    for k, (n, rows) in enumerate(parts):
        here = view(held[n], rows)
        fetch.append(pltpu.make_async_copy(view(ins[n], rows), here, sem_in.at[k]))
        store.append(pltpu.make_async_copy(here, view(outs[n], rows), sem_out.at[k]))
    for copy in fetch:
        copy.start()
    for first, second in zip(fetch, store):
        first.wait()
        second.start()
    for copy in store:
        copy.wait()


def local(queries, key_rows, value_rows, upstream, head_gate, slot_heads):
    vmem = pl.BlockSpec(memory_space=pltpu.VMEM)
    smem = pl.BlockSpec(memory_space=pltpu.SMEM)
    hbm = pl.BlockSpec(memory_space=pl.ANY)
    dma = pltpu.SemaphoreType.DMA
    out_shape = (
        jax.ShapeDtypeStruct(queries.shape, BF16),
        jax.ShapeDtypeStruct(key_rows.shape, BF16),
        jax.ShapeDtypeStruct(value_rows.shape, BF16),
        jax.ShapeDtypeStruct(head_gate.shape, F32),
    )
    half = KV_COLS // 2
    rows_of_pair = pltpu.VMEM((PAIRS, SEQ, 128), BF16)
    results = pl.pallas_call(
        kernel,
        out_shape=out_shape,
        in_specs=[smem, smem, hbm, hbm, vmem, vmem],
        out_specs=(hbm, vmem, vmem, smem),
        scratch_shapes=[
            pltpu.VMEM((2, 4, 2, 4, CHIP, half), BF16),
            pltpu.VMEM((SEQ, KV_COLS), BF16),
            pltpu.VMEM((Q_COLS, KV_COLS), BF16),
            rows_of_pair, rows_of_pair,
            pltpu.VMEM((PAIRS, 128, SEQ), BF16),
            rows_of_pair, rows_of_pair, rows_of_pair, rows_of_pair, rows_of_pair, rows_of_pair,
            pltpu.VMEM((2, SEQ, BLK), F32),
            pltpu.VMEM((HEADS, SEQ, SEQ), BF16),
            pltpu.VMEM((HEADS, SEQ, SEQ), BF16),
            pltpu.VMEM((HEADS, 8, SEQ), F32),
            pltpu.VMEM((2, 8, 128), F32),
            pltpu.VMEM((2, 3, 8, 128), F32),
            pltpu.VMEM((2, 4, 2, 4, CHIP, half), BF16),
            pltpu.VMEM((2, 4, 4, CHIP, half), BF16),
            pltpu.VMEM((2, 4, 4, CHIP, half), BF16),
            pltpu.VMEM((2, 4, 4, CHIP, half), BF16),
            pltpu.VMEM((2, 4, CHIP, half), BF16),
            pltpu.VMEM((2, 4, CHIP, half), BF16),
            dma((2, PAIRS)), dma((NBLK, PAIRS)),
            dma((2, 3)), dma((2, 4)), dma((2, 4, 3)), dma((2, 4, 4)), dma((2, 4)), dma((2, 4)),
            dma((2, 4)), dma((2, 4)), dma((2, 4)), dma((2, 4)), dma((2, 3)), dma((2, 4)),
            dma((2, 3)), dma((2, 3)), pltpu.SemaphoreType.REGULAR((3,)),
        ],
        compiler_params=pltpu.CompilerParams(
            collective_id=0, has_side_effects=True, vmem_limit_bytes=58 * 1024 * 1024
        ),
        name="attention_backward",
    )(slot_heads, head_gate, queries, upstream, key_rows, value_rows)
    return pl.pallas_call(
        finish,
        out_shape=out_shape,
        in_specs=[hbm] * 4,
        out_specs=(hbm,) * 4,
        scratch_shapes=[
            pltpu.VMEM(queries.shape, BF16),
            pltpu.VMEM(key_rows.shape, BF16),
            pltpu.VMEM(value_rows.shape, BF16),
            pltpu.SMEM(head_gate.shape, F32),
            dma((6,)), dma((6,)),
        ],
        name="copy_out",
    )(*results)


def solution(mesh):
    in_specs = (
        P("dp", None, "head"),
        P("dp", "head", None),
        P("dp", "head", None),
        P("dp", None, "head"),
        P("head"),
        P("head"),
    )
    out_specs = (P("dp", None, "head"), P("dp", "head", None), P("dp", "head", None), P("head"))
    return jax.shard_map(local, mesh=mesh, in_specs=in_specs, out_specs=out_specs, check_vma=False)
```

time: 70.3 us -> 54.9 us (0.78); the launches traced: 69.3 us -> 54.7 us
  Pallas kernels: 64.9 us -> 54.1 us
  local copies, waits for them, and re-layouts: 3.84 us -> 0 us
    pallas_call x1 -> x2, Pallas kernels: 64.9 us -> 54.1 us  [the longest x1 52.2 us: local(): pl.pallas_call(kernel, out_shape=out_shape, in_specs=[smem, smem, hbm, hb...]
    unnamed x10 -> x0, local copies, waits for them, and re-layouts: 3.84 us -> none
where the time goes in v2:
time: 54.9 us; the launch traced here: 54.7 us
  Pallas kernels  54.1 us (99%)
  between operations  0.64 us (1%)
    pallas_call x1, Pallas kernels, local(): pl.pallas_call(kernel, out_shape=out_shape, in_specs=[smem, smem, hbm, hb...  52.2 us
    pallas_call x1, Pallas kernels, local(): pl.pallas_call(finish, out_shape=out_shape, in_specs=[hbm] * 4, out_specs...  1.91 us

profile of v2, /device:TPU:1, one launch (start us, length us, event | category | flops | bytes accessed | tf_op | source)
XLA Modules:
  0.0 54.7 jit_solution(256633507491143687)
XLA Ops:
  0.6 52.2 %attention_backward.1 = (bf16[1,768,384]{2,1,0:T(8,128)(2,1)}, bf16[1,24,512]{2,1,0:T(8,128)(2,1)}, bf16[1,24,512]{2,1,0:T(8,128)(2,1)}, f32[6]{0:T(128)}) custom-call(s32[6]{0:T(128)} %slots.1, f32[6]{0:T(128)} %gates.1, bf16[1,768,384]{2,1,0:T(8,128)(2,1)} %q_hbm.1, bf16[1,768,384]{2,1,0:T(8,128)(2,1)} %dy_hbm.1, bf16[1,24,512]{2,1,0:T(8,128)(2,1)} %key_ref.1, ...), custom_call_target="tpu_custom_call" | custom-call | tf_op jit(solution)/shard_map/attention_backward/pallas_call | solution.py:493
  52.8 1.9 %copy_out.1 = (bf16[1,768,384]{2,1,0:T(8,128)(2,1)}, bf16[1,24,512]{2,1,0:T(8,128)(2,1)}, bf16[1,24,512]{2,1,0:T(8,128)(2,1)}, f32[6]{0:T(128)}) custom-call(bf16[1,768,384]{2,1,0:T(8,128)(2,1)} %get-tuple-element.8.refs_0_, bf16[1,24,512]{2,1,0:T(8,128)(2,1)} %get-tuple-element.9.refs_1_, bf16[1,24,512]{2,1,0:T(8,128)(2,1)} %get-tuple-element.10.refs_2_, ...), custom_call_target="tpu_custom_call" | custom-call | tf_op jit(solution)/shard_map/copy_out/pallas_call | solution.py:527

commit v3 on v2

--- a/solution.py
+++ b/solution.py
@@ -56,10 +56,10 @@
     slots, gates, q_hbm, dy_hbm, key_ref, value_ref,
     dq_hbm, dk_ref, dv_ref, gg_ref,
     shards, k_all, sel_t, k_sel, v_sel, k_sel_t, q_ref, dy_ref, dyg_ref, qn_ref, dyn_ref, dq_ref,
-    s_ref, p_ref, ds_ref, scale_ref, gate_acc, gate_recv,
-    part, part_recv, chip_sum, x_recv, x_sum, z_recv,
+    s_ref, p_ref, dp_ref, ds_ref, scale_ref, delta_ref, gate_acc, gate_recv,
+    part, part_recv, chip_sum, x_recv, x_sum, z_recv, first_recv, first_sum, first_x_recv,
     load_sem, store_sem, agz_send, agz_recv, agx_send, agx_recv, agc_send, agc_recv,
-    c_send, c_recv, x_send, x_recv_sem, z_send, z_recv_sem, g_send, g_recv, go,
+    c_send, c_recv, x_send, x_recv_sem, z_send, z_recv_sem, g_send, g_recv, fz_send, fz_recv, fx_send, fx_recv, go,
 ):
     me = lax.axis_index("head")
     x, z, c = me // 8, (me // 2) % 4, me % 2
@@ -151,17 +151,6 @@
 
     send_z(KEY)
     send_x(KEY, 0, z)
-    send_z(VALUE)
-    forward_z(KEY)
-    send_x(VALUE, 0, z)
-    forward_z(VALUE)
-
-    for d in (1, 2, 3):
-        pl.when((zh + d) % 4 < zh)(
-            lambda d=d: pl.semaphore_signal(
-                go.at[3 - d], inc=1, device_id=dp_id(y, (zh + d) % 4), device_id_type=MESH
-            )
-        )
 
     row = lax.broadcasted_iota(jnp.int32, (Q_COLS, KV_COLS), 0)
     col = lax.broadcasted_iota(jnp.int32, (Q_COLS, KV_COLS), 1)
@@ -171,6 +160,9 @@
         group_of_row = jnp.where(slot_of_row == h, slots[h] // GROUP_HEADS, group_of_row)
     wanted = group_of_row * HEAD_DIM + row % HEAD_DIM
     sel_t[...] = jnp.where(col == wanted, 1.0, 0.0).astype(BF16)
+
+    forward_z(KEY)
+    send_z(VALUE)
 
     for load in loads:
         load.wait()
@@ -196,6 +188,15 @@
             target[p, rows, :] = chosen[:, p * 128 : (p + 1) * 128]
 
     forward_x(KEY)
+    send_x(VALUE, 0, z)
+    forward_z(VALUE)
+    for d in (1, 2, 3):
+        pl.when((zh + d) % 4 < zh)(
+            lambda d=d: pl.semaphore_signal(
+                go.at[3 - d], inc=1, device_id=dp_id(y, (zh + d) % 4), device_id_type=MESH
+            )
+        )
+
     for d in (0, 1, 3, 2):
         select_x(KEY, (x + d) % 4)
 
@@ -247,22 +248,23 @@
         for j in range(i + 1):
             keys = pl.ds(BLK * j, BLK)
             dp = dot_t(v_sel[p, keys, :], dy_half)
-            s_ref[half, keys, :] = dp
+            dp_ref[h, keys, queries] = dp
             weighted = weighted + fold(p_ref[h, keys, queries].astype(F32) * dp, jnp.sum)
         delta = jnp.sum(weighted, axis=0, keepdims=True) * scale_ref[h, 0:1, queries]
+        delta_ref[h, :, queries] = jnp.broadcast_to(delta, (8, BLK))
         gate_acc[0, h : h + 1, :] = (
             gate_acc[0, h : h + 1, :] + delta[:, 0:128] + delta[:, 128:256]
         )
-        return delta
-
-    def score_grad(i, p, half, delta):
+
+    def score_grad(i, p, half):
         queries = pl.ds(BLK * i, BLK)
         h = 2 * p + half
         depth = BLK * (i + 1)
+        delta = delta_ref[h, 0:1, queries]
         for k0 in range(0, depth, STEP):
             keys = pl.ds(k0, STEP)
             ds_ref[h, keys, queries] = (
-                p_ref[h, keys, queries].astype(F32) * (s_ref[half, keys, :] - delta)
+                p_ref[h, keys, queries].astype(F32) * (dp_ref[h, keys, queries] - delta)
             ).astype(BF16)
 
     def query_grad_t(i, p, half):
@@ -276,9 +278,8 @@
     def grad_block(i):
         queries = pl.ds(BLK * i, BLK)
         for p in range(PAIRS):
-            deltas = [weight_grad(i, p, half) for half in range(2)]
             for half in range(2):
-                score_grad(i, p, half, deltas[half])
+                score_grad(i, p, half)
             dq_t = [query_grad_t(i, p, half) for half in range(2)]
             dq_ref[p, queries, :] = jnp.concatenate(dq_t, axis=0).T.astype(BF16)
 
@@ -351,9 +352,11 @@
                 part[t, xx, c, zz].astype(F32) + part_recv[t, xx, zz].astype(F32)
             ).astype(BF16)
 
-        @pl.when(xx != x)
-        def _():
-            x_copy(t, xx).start()
+        if (t, xx) != (KEY, 0):
+
+            @pl.when(xx != x)
+            def _():
+                x_copy(t, xx).start()
 
     def x_add(t):
         for d in (1, 3, 2):
@@ -368,7 +371,9 @@
             for dx in (1, 2, 3):
                 total = total + x_recv[t, (x + dx) % 4, zz].astype(F32)
             x_sum[t, zz] = total.astype(BF16)
-            if slot < 3:
+            if slot < 3 and t == KEY:
+                z_copy(t, slot, zz).start()
+            elif slot < 3:
                 send(z_copy(t, slot, zz))
 
     def z_add(t, out_ref):
@@ -382,6 +387,27 @@
             total = total + z_recv[t, zz].astype(F32)
         out_ref[0] = unpack_rows(total).astype(BF16)
 
+    def first_z_copy(slot, zz):
+        return pltpu.make_async_remote_copy(
+            src_ref=chip_sum.at[KEY, 0, zz], dst_ref=first_recv.at[z],
+            send_sem=fz_send.at[slot], recv_sem=fz_recv.at[z],
+            device_id=head_id(x, zz, c), device_id_type=MESH,
+        )
+
+    def first_z_wait(slot, zz):
+        pltpu.make_async_remote_copy(
+            src_ref=chip_sum.at[KEY, 0, zz], dst_ref=first_recv.at[zz],
+            send_sem=fz_send.at[slot], recv_sem=fz_recv.at[zz],
+            device_id=head_id(x, zz, c), device_id_type=MESH,
+        ).wait_recv()
+
+    def first_x_copy(xx):
+        return pltpu.make_async_remote_copy(
+            src_ref=first_sum, dst_ref=first_x_recv.at[xx],
+            send_sem=fx_send.at[0], recv_sem=fx_recv.at[xx],
+            device_id=head_id(0, z, c), device_id_type=MESH,
+        )
+
     def gate_copy(stage, d, target):
         return pltpu.make_async_remote_copy(
             src_ref=gate_acc.at[stage], dst_ref=gate_recv.at[stage, d - 1],
@@ -406,18 +432,30 @@
     forward_x(VALUE)
     score_block(0)
     chip_add(VALUE, 2)
-    key_block(VALUE, 1)
-    key_block(VALUE, 0)
 
     k_sel_t_all = dot_t(sel_t[...], k_all[...]).astype(BF16)
     for p in range(PAIRS):
         k_sel_t[p] = k_sel_t_all[p * 128 : (p + 1) * 128, :]
     for d in (0, 1, 3, 2):
         select_x(VALUE, (x + d) % 4)
+    for i in (2, 1, 0):
+        for p in range(PAIRS):
+            for half in range(2):
+                weight_grad(i, p, half)
+
+    for d in (1, 2, 3):
+        send(gate_copy(0, d, dp_id((y + d) % 4, zh)))
+    key_block(VALUE, 1)
+    key_block(VALUE, 0)
     chip_add(VALUE, 1)
+    gate_acc[1] = gate_add(0)
+    for d in (1, 2, 3):
+        pl.when((zh + d) % 4 > zh)(lambda d=d: pl.semaphore_wait(go.at[d - 1], 1))
+    for d in (1, 2, 3):
+        send(gate_copy(1, d, dp_id(y, (zh + d) % 4)))
+
+    grad_block(2)
     chip_add(VALUE, 0)
-
-    grad_block(2)
     key_block(KEY, 3)
     store_queries(2)
     grad_block(1)
@@ -425,30 +463,47 @@
     key_block(KEY, 2)
     store_queries(1)
     grad_block(0)
-    for d in (1, 2, 3):
-        send(gate_copy(0, d, dp_id((y + d) % 4, zh)))
     chip_add(KEY, 2)
     key_block(KEY, 1)
     store_queries(0)
     key_block(KEY, 0)
     chip_add(KEY, 1)
-    gate_acc[1] = gate_add(0)
-    for d in (1, 2, 3):
-        pl.when((zh + d) % 4 > zh)(lambda d=d: pl.semaphore_wait(go.at[d - 1], 1))
-    for d in (1, 2, 3):
-        send(gate_copy(1, d, dp_id(y, (zh + d) % 4)))
     chip_add(KEY, 0)
+    for slot, zz in enumerate(near):
+        send(first_z_copy(slot, zz))
     x_add(VALUE)
+    first = chip_sum[KEY, 0, z].astype(F32)
+    for slot, zz in enumerate(near):
+        first_z_wait(slot, zz)
+        first = first + first_recv[zz].astype(F32)
+    first_sum[...] = first.astype(BF16)
+
+    @pl.when(x != 0)
+    def _():
+        first_x_copy(x).start()
+        x_add(KEY)
+        z_add(KEY, dk_ref)
+        for slot, zz in enumerate(near):
+            z_copy(KEY, slot, zz).wait_send()
+        first_x_copy(x).wait_send()
+
+    @pl.when(x == 0)
+    def _():
+        total = first_sum[...].astype(F32)
+        for xx in (3, 1, 2):
+            first_x_copy(xx).wait_recv()
+            total = total + first_x_recv[xx].astype(F32)
+        dk_ref[0] = unpack_rows(total).astype(BF16)
+
     z_add(VALUE, dv_ref)
-    x_add(KEY)
-    z_add(KEY, dk_ref)
     gate_sum = gate_add(1)
     for h in range(HEADS):
         gg_ref[h] = jnp.sum(gate_sum[h : h + 1, :]) / (16.0 * gates[h])
 
-    for t in (KEY, VALUE):
-        for d in (1, 2, 3):
-            x_copy(t, (x + d) % 4).wait_send()
+    for xx in range(4):
+        for t in (KEY, VALUE):
+            if (t, xx) != (KEY, 0):
+                pl.when(xx != x)(lambda t=t, xx=xx: x_copy(t, xx).wait_send())
     for copy in sends:
         copy.wait_send()
     for copy in stores:
@@ -504,7 +559,9 @@
             rows_of_pair, rows_of_pair, rows_of_pair, rows_of_pair, rows_of_pair, rows_of_pair,
             pltpu.VMEM((2, SEQ, BLK), F32),
             pltpu.VMEM((HEADS, SEQ, SEQ), BF16),
+            pltpu.VMEM((HEADS, SEQ, SEQ), F32),
             pltpu.VMEM((HEADS, SEQ, SEQ), BF16),
+            pltpu.VMEM((HEADS, 8, SEQ), F32),
             pltpu.VMEM((HEADS, 8, SEQ), F32),
             pltpu.VMEM((2, 8, 128), F32),
             pltpu.VMEM((2, 3, 8, 128), F32),
@@ -514,10 +571,14 @@
             pltpu.VMEM((2, 4, 4, CHIP, half), BF16),
             pltpu.VMEM((2, 4, CHIP, half), BF16),
             pltpu.VMEM((2, 4, CHIP, half), BF16),
+            pltpu.VMEM((4, CHIP, half), BF16),
+            pltpu.VMEM((CHIP, half), BF16),
+            pltpu.VMEM((4, CHIP, half), BF16),
             dma((2, PAIRS)), dma((NBLK, PAIRS)),
             dma((2, 3)), dma((2, 4)), dma((2, 4, 3)), dma((2, 4, 4)), dma((2, 4)), dma((2, 4)),
             dma((2, 4)), dma((2, 4)), dma((2, 4)), dma((2, 4)), dma((2, 3)), dma((2, 4)),
-            dma((2, 3)), dma((2, 3)), pltpu.SemaphoreType.REGULAR((3,)),
+            dma((2, 3)), dma((2, 3)), dma((3,)), dma((4,)), dma((1,)), dma((4,)),
+            pltpu.SemaphoreType.REGULAR((3,)),
         ],
         compiler_params=pltpu.CompilerParams(
             collective_id=0, has_side_effects=True, vmem_limit_bytes=58 * 1024 * 1024

time: 54.9 us -> 51.1 us (0.931); the launches traced: 54.7 us -> 50.2 us
  Pallas kernels: 54.1 us -> 49.4 us
    pallas_call x1, Pallas kernels: 52.2 us -> 47.4 us  [local(): pl.pallas_call(kernel, out_shape=out_shape, in_specs=[smem, smem, hbm, hb...]
where the time goes in v3:
time: 51.1 us; the launch traced here: 50.2 us
  Pallas kernels  49.4 us (97%)
  between operations  0.8 us (2%)
    pallas_call x1, Pallas kernels, local(): pl.pallas_call(kernel, out_shape=out_shape, in_specs=[smem, smem, hbm, hb...  47.4 us
    pallas_call x1, Pallas kernels, local(): pl.pallas_call(finish, out_shape=out_shape, in_specs=[hbm] * 4, out_specs...  1.91 us

profile of v3, /device:TPU:1, one launch (start us, length us, event | category | flops | bytes accessed | tf_op | source)
XLA Modules:
  0.0 50.2 jit_solution(2012398625759584207)
XLA Ops:
  0.6 47.4 %attention_backward.1 = (bf16[1,768,384]{2,1,0:T(8,128)(2,1)}, bf16[1,24,512]{2,1,0:T(8,128)(2,1)}, bf16[1,24,512]{2,1,0:T(8,128)(2,1)}, f32[6]{0:T(128)}) custom-call(s32[6]{0:T(128)} %slots.1, f32[6]{0:T(128)} %gates.1, bf16[1,768,384]{2,1,0:T(8,128)(2,1)} %q_hbm.1, bf16[1,768,384]{2,1,0:T(8,128)(2,1)} %dy_hbm.1, bf16[1,24,512]{2,1,0:T(8,128)(2,1)} %key_ref.1, ...), custom_call_target="tpu_custom_call" | custom-call | tf_op jit(solution)/shard_map/attention_backward/pallas_call | solution.py:548
  48.1 1.9 %copy_out.1 = (bf16[1,768,384]{2,1,0:T(8,128)(2,1)}, bf16[1,24,512]{2,1,0:T(8,128)(2,1)}, bf16[1,24,512]{2,1,0:T(8,128)(2,1)}, f32[6]{0:T(128)}) custom-call(bf16[1,768,384]{2,1,0:T(8,128)(2,1)} %get-tuple-element.8.refs_0_, bf16[1,24,512]{2,1,0:T(8,128)(2,1)} %get-tuple-element.9.refs_1_, bf16[1,24,512]{2,1,0:T(8,128)(2,1)} %get-tuple-element.10.refs_2_, ...), custom_call_target="tpu_custom_call" | custom-call | tf_op jit(solution)/shard_map/copy_out/pallas_call | solution.py:588

commit v4 on v3

--- a/solution.py
+++ b/solution.py
@@ -53,10 +53,11 @@
 
 
 def kernel(
-    slots, gates, q_hbm, dy_hbm, key_ref, value_ref,
-    dq_hbm, dk_ref, dv_ref, gg_ref,
+    slots_hbm, gates_hbm, q_hbm, dy_hbm, key_hbm, value_hbm,
+    dq_hbm, dk_hbm, dv_hbm, gg_hbm,
+    slots, gates, key_ref, value_ref, dk_ref, dv_ref, gg_ref, small_in, small_out,
     shards, k_all, sel_t, k_sel, v_sel, k_sel_t, q_ref, dy_ref, dyg_ref, qn_ref, dyn_ref, dq_ref,
-    s_ref, p_ref, dp_ref, ds_ref, scale_ref, delta_ref, gate_acc, gate_recv,
+    p_ref, dp_ref, ds_ref, scale_ref, delta_ref, gate_acc, gate_recv,
     part, part_recv, chip_sum, x_recv, x_sum, z_recv, first_recv, first_sum, first_x_recv,
     load_sem, store_sem, agz_send, agz_recv, agx_send, agx_recv, agc_send, agc_recv,
     c_send, c_recv, x_send, x_recv_sem, z_send, z_recv_sem, g_send, g_recv, fz_send, fz_recv, fx_send, fx_recv, go,
@@ -75,6 +76,15 @@
     sibling = head_id(x, z, 1 - c)
     near = (z + 1 - 2 * (z % 2), 2 - z // 2, 3 - 3 * (z // 2))
 
+    fetches = [
+        pltpu.make_async_copy(there, here, small_in.at[n])
+        for n, (there, here) in enumerate(
+            ((key_hbm, key_ref), (value_hbm, value_ref), (slots_hbm, slots), (gates_hbm, gates))
+        )
+    ]
+    for fetch in fetches:
+        fetch.start()
+
     barrier = pltpu.get_barrier_semaphore()
 
     def greet(target):
@@ -96,6 +106,8 @@
     for load in loads:
         load.start()
 
+    for fetch in fetches:
+        fetch.wait()
     shards[KEY, x, c, z] = pack_rows(key_ref[0].astype(F32)).astype(BF16)
     shards[VALUE, x, c, z] = pack_rows(value_ref[0].astype(F32)).astype(BF16)
 
@@ -215,7 +227,7 @@
             if j == i:
                 s = jnp.where(causal, s, NEG)
             top = jnp.maximum(top, fold(s, jnp.max))
-            s_ref[half, keys, :] = s
+            dp_ref[2 * p + half, keys, queries] = s
         return jnp.max(top, axis=0, keepdims=True) * SCALE_LOG2
 
     def exp_block(i, p, half, top):
@@ -224,7 +236,7 @@
         total = jnp.zeros((8, BLK), F32)
         for k0 in range(0, BLK * (i + 1), STEP):
             keys = pl.ds(k0, STEP)
-            e = jnp.exp2(s_ref[half, keys, :] * SCALE_LOG2 - top)
+            e = jnp.exp2(dp_ref[h, keys, queries] * SCALE_LOG2 - top)
             total = total + fold(e, jnp.sum)
             p_ref[h, keys, queries] = e.astype(BF16)
         inverse = 1.0 / jnp.sum(total, axis=0, keepdims=True)
@@ -429,8 +441,8 @@
     score_block(1)
     chip_add(VALUE, 3)
     key_block(VALUE, 2)
+    score_block(0)
     forward_x(VALUE)
-    score_block(0)
     chip_add(VALUE, 2)
 
     k_sel_t_all = dot_t(sel_t[...], k_all[...]).astype(BF16)
@@ -478,10 +490,25 @@
         first = first + first_recv[zz].astype(F32)
     first_sum[...] = first.astype(BF16)
 
+    def store_small(n, here, there):
+        copy = pltpu.make_async_copy(here, there, small_out.at[n])
+        copy.start()
+        stores.append(copy)
+
     @pl.when(x != 0)
     def _():
         first_x_copy(x).start()
         x_add(KEY)
+
+    z_add(VALUE, dv_ref)
+    store_small(0, dv_ref, dv_hbm)
+    gate_sum = gate_add(1)
+    for h in range(HEADS):
+        gg_ref[h] = jnp.sum(gate_sum[h : h + 1, :]) / (16.0 * gates[h])
+    store_small(1, gg_ref, gg_hbm)
+
+    @pl.when(x != 0)
+    def _():
         z_add(KEY, dk_ref)
         for slot, zz in enumerate(near):
             z_copy(KEY, slot, zz).wait_send()
@@ -495,11 +522,7 @@
             total = total + first_x_recv[xx].astype(F32)
         dk_ref[0] = unpack_rows(total).astype(BF16)
 
-    z_add(VALUE, dv_ref)
-    gate_sum = gate_add(1)
-    for h in range(HEADS):
-        gg_ref[h] = jnp.sum(gate_sum[h : h + 1, :]) / (16.0 * gates[h])
-
+    store_small(2, dk_ref, dk_hbm)
     for xx in range(4):
         for t in (KEY, VALUE):
             if (t, xx) != (KEY, 0):
@@ -533,8 +556,6 @@
 
 
 def local(queries, key_rows, value_rows, upstream, head_gate, slot_heads):
-    vmem = pl.BlockSpec(memory_space=pltpu.VMEM)
-    smem = pl.BlockSpec(memory_space=pltpu.SMEM)
     hbm = pl.BlockSpec(memory_space=pl.ANY)
     dma = pltpu.SemaphoreType.DMA
     out_shape = (
@@ -548,16 +569,23 @@
     results = pl.pallas_call(
         kernel,
         out_shape=out_shape,
-        in_specs=[smem, smem, hbm, hbm, vmem, vmem],
-        out_specs=(hbm, vmem, vmem, smem),
+        in_specs=[hbm] * 6,
+        out_specs=(hbm,) * 4,
         scratch_shapes=[
+            pltpu.SMEM(slot_heads.shape, jnp.int32),
+            pltpu.SMEM(head_gate.shape, F32),
+            pltpu.VMEM(key_rows.shape, BF16),
+            pltpu.VMEM(value_rows.shape, BF16),
+            pltpu.VMEM(key_rows.shape, BF16),
+            pltpu.VMEM(value_rows.shape, BF16),
+            pltpu.SMEM(head_gate.shape, F32),
+            dma((4,)), dma((3,)),
             pltpu.VMEM((2, 4, 2, 4, CHIP, half), BF16),
             pltpu.VMEM((SEQ, KV_COLS), BF16),
             pltpu.VMEM((Q_COLS, KV_COLS), BF16),
             rows_of_pair, rows_of_pair,
             pltpu.VMEM((PAIRS, 128, SEQ), BF16),
             rows_of_pair, rows_of_pair, rows_of_pair, rows_of_pair, rows_of_pair, rows_of_pair,
-            pltpu.VMEM((2, SEQ, BLK), F32),
             pltpu.VMEM((HEADS, SEQ, SEQ), BF16),
             pltpu.VMEM((HEADS, SEQ, SEQ), F32),
             pltpu.VMEM((HEADS, SEQ, SEQ), BF16),

time: 51.1 us -> 50.1 us (0.980)
  Pallas kernels: 49.4 us -> 48.4 us
    pallas_call x1, Pallas kernels: 47.4 us -> 46.5 us  [local(): pl.pallas_call(kernel, out_shape=out_shape, in_specs=[hbm] * 6, out_specs...]
where the time goes in v4:
time: 50.1 us; the launch traced here: 49.2 us
  Pallas kernels  48.4 us (97%)
  between operations  0.8 us (2%)
    pallas_call x1, Pallas kernels, local(): pl.pallas_call(kernel, out_shape=out_shape, in_specs=[hbm] * 6, out_specs...  46.5 us
    pallas_call x1, Pallas kernels, local(): pl.pallas_call(finish, out_shape=out_shape, in_specs=[hbm] * 4, out_specs...  1.91 us

profile of v4, /device:TPU:1, one launch (start us, length us, event | category | flops | bytes accessed | tf_op | source)
XLA Modules:
  0.0 49.2 jit_solution(6780668832606998185)
XLA Ops:
  0.6 46.5 %attention_backward.1 = (bf16[1,768,384]{2,1,0:T(8,128)(2,1)}, bf16[1,24,512]{2,1,0:T(8,128)(2,1)}, bf16[1,24,512]{2,1,0:T(8,128)(2,1)}, f32[6]{0:T(128)}) custom-call(s32[6]{0:T(128)} %slots_hbm.1, f32[6]{0:T(128)} %gates_hbm.1, bf16[1,768,384]{2,1,0:T(8,128)(2,1)} %q_hbm.1, bf16[1,768,384]{2,1,0:T(8,128)(2,1)} %dy_hbm.1, bf16[1,24,512]{2,1,0:T(8,128)(2,1)} %key_hbm.1, ...), custom_call_target="tpu_custom_call" | custom-call | tf_op jit(solution)/shard_map/attention_backward/pallas_call | solution.py:569
  47.1 1.9 %copy_out.1 = (bf16[1,768,384]{2,1,0:T(8,128)(2,1)}, bf16[1,24,512]{2,1,0:T(8,128)(2,1)}, bf16[1,24,512]{2,1,0:T(8,128)(2,1)}, f32[6]{0:T(128)}) custom-call(bf16[1,768,384]{2,1,0:T(8,128)(2,1)} %get-tuple-element.8.refs_0_, bf16[1,24,512]{2,1,0:T(8,128)(2,1)} %get-tuple-element.9.refs_1_, bf16[1,24,512]{2,1,0:T(8,128)(2,1)} %get-tuple-element.10.refs_2_, ...), custom_call_target="tpu_custom_call" | custom-call | tf_op jit(solution)/shard_map/copy_out/pallas_call | solution.py:616
